TPU v7x, 32 devices: a whole 2x2x4 slice. The times are simulated.
32 devices in a mesh: seq: 8 (over z, x), text: 4 (over y, core).
Axes of the slice: x: 2, y: 2, z: 4, core: 2. Of those that a mesh axis runs over, the one named last changes fastest.
Arguments:
- queries: bfloat16 [24576, 4096], P('seq', 'text'), may hold values from -2.5 to 2.5
- keys: bfloat16 [28672, 4096], P('text', 'seq'), may hold values from -2.5 to 2.5
- values: bfloat16 [28672, 4096], P('text', 'seq'), may hold values from -6 to 6
- grad_out: bfloat16 [24576, 4096], P('seq', 'text'), may hold values from -6 to 6
- res_len: int32 [64], replicated, may hold values from 1 to 384, 15360 in all
- tok_len: int32 [64], replicated, may hold values from 1 to 448, 17920 in all
Outputs:
- grad_queries: bfloat16 [24576, 4096], P('seq', 'text')
- grad_keys: bfloat16 [28672, 4096], P('text', 'seq')
- grad_values: bfloat16 [28672, 4096], P('text', 'seq')
Inputs may be any that keep to these rules, and one draw needn't show every extreme that they name: Residue rows p * 384 + i with i >= res_len[p] are padding. Token rows of slot u(p) at positions j >= tok_len[p] are padding.
All inputs are finite; a program needn't handle non-finite values.
Results may differ from a plain program's by a relative error of at most 0.0054.
Values may be sent and summed in bfloat16 or wider, within the bound.
A program may use at most 128 MiB of HBM per device.

v0:
```python
import math

import jax
import jax.numpy as jnp
from jax import lax
from jax.sharding import PartitionSpec as P

HEAD_DIM = 128
RES_TILES = 3
TOK_TILES = 7


def local_backward(queries, grad_out, keys, values, live_rows, live_tokens):
    res_slot = RES_TILES * 128
    tok_slot = TOK_TILES * 64
    feature_width = queries.shape[1]
    heads_here = feature_width // HEAD_DIM
    proteins_here = live_rows.shape[0]
    group = 2
    groups = proteins_here // group
    softmax_scale = 1.0 / math.sqrt(HEAD_DIM)
    row_index = jnp.arange(res_slot, dtype=jnp.int32)
    col_index = jnp.arange(tok_slot, dtype=jnp.int32)

    def per_group(carry, packed):
        query_part, grad_part, key_part, value_part, rows_live, tokens_live = packed
        col_ok = col_index[None, :] < tokens_live[:, None]
        row_ok = row_index[None, :] < rows_live[:, None]
        scores = (
            jnp.einsum("grhd,gthd->ghrt", query_part, key_part, preferred_element_type=jnp.float32)
            * softmax_scale
        )
        raised = jnp.where(col_ok[:, None, None, :], jnp.exp(scores), 0.0)
        total = jnp.sum(raised, axis=-1, keepdims=True)
        attention = jnp.where(row_ok[:, None, :, None], raised / total, 0.0)
        attention_b = attention.astype(jnp.bfloat16)
        output = jnp.einsum(
            "ghrt,gthd->grhd", attention_b, value_part, preferred_element_type=jnp.float32
        )
        delta = jnp.sum(grad_part.astype(jnp.float32) * output, axis=-1).transpose(0, 2, 1)
        grad_attention = jnp.einsum(
            "grhd,gthd->ghrt", grad_part, value_part, preferred_element_type=jnp.float32
        )
        scores_b = (softmax_scale * attention * (grad_attention - delta[:, :, :, None])).astype(
            jnp.bfloat16
        )
        query_grad = jnp.einsum(
            "ghrt,gthd->grhd", scores_b, key_part, preferred_element_type=jnp.float32
        ).astype(jnp.bfloat16)
        key_grad = jnp.einsum(
            "ghrt,grhd->gthd", scores_b, query_part, preferred_element_type=jnp.float32
        ).astype(jnp.bfloat16)
        value_grad = jnp.einsum(
            "ghrt,grhd->gthd", attention_b, grad_part, preferred_element_type=jnp.float32
        ).astype(jnp.bfloat16)
        return (carry, (query_grad, key_grad, value_grad))

    shaped = (
        queries.reshape(groups, group, res_slot, heads_here, HEAD_DIM),
        grad_out.reshape(groups, group, res_slot, heads_here, HEAD_DIM),
        keys.reshape(groups, group, tok_slot, heads_here, HEAD_DIM),
        values.reshape(groups, group, tok_slot, heads_here, HEAD_DIM),
        live_rows.reshape(groups, group),
        live_tokens.reshape(groups, group),
    )
    unused, (query_grads, key_grads, value_grads) = lax.scan(
        per_group, jnp.zeros((), jnp.float32), shaped
    )
    return (
        query_grads.reshape(queries.shape),
        key_grads.reshape(keys.shape),
        value_grads.reshape(values.shape),
    )


def body(queries, keys, values, grad_out, res_len, tok_len):
    text_ways = lax.axis_size("text")
    res_slot = RES_TILES * 128
    tok_slot = TOK_TILES * 64
    prot_seq = queries.shape[0] // res_slot
    feature_width = queries.shape[1]

    def by_block(field):
        return (
            field.reshape(prot_seq // text_ways, text_ways, res_slot, feature_width)
            .transpose(1, 0, 2, 3)
            .reshape(-1, feature_width)
        )

    middle_queries, middle_grads = (
        lax.all_to_all(by_block(queries), "text", split_axis=0, concat_axis=1, tiled=True),
        lax.all_to_all(by_block(grad_out), "text", split_axis=0, concat_axis=1, tiled=True),
    )
    far_queries, far_grads = (
        lax.all_to_all(middle_queries, "seq", split_axis=1, concat_axis=0, tiled=True),
        lax.all_to_all(middle_grads, "seq", split_axis=1, concat_axis=0, tiled=True),
    )
    text_block = lax.axis_index("text")
    proteins_here = keys.shape[0] // tok_slot
    live_rows = lax.dynamic_index_in_dim(
        res_len.reshape(proteins_here, text_ways), text_block, 1, keepdims=False
    )
    live_tokens = lax.dynamic_index_in_dim(
        tok_len.reshape(proteins_here, text_ways), text_block, 1, keepdims=False
    )
    far_query_grads, key_grads, value_grads = local_backward(
        far_queries, far_grads, keys, values, live_rows, live_tokens
    )
    returned = lax.all_to_all(
        lax.all_to_all(far_query_grads, "seq", split_axis=0, concat_axis=1, tiled=True),
        "text",
        split_axis=1,
        concat_axis=0,
        tiled=True,
    )
    query_grads = (
        returned.reshape(text_ways, prot_seq // text_ways, res_slot, feature_width)
        .transpose(1, 0, 2, 3)
        .reshape(-1, feature_width)
    )
    return (query_grads, key_grads, value_grads)


def solution(mesh):
    return jax.shard_map(
        body,
        mesh=mesh,
        in_specs=(P("seq", "text"), P("text", "seq"), P("text", "seq"), P("seq", "text"), P(), P()),
        out_specs=(P("seq", "text"), P("text", "seq"), P("text", "seq")),
        check_vma=False,
    )
```

profile of v0, /device:TPU:14, one launch (start us, length us, event | category | flops | bytes accessed | tf_op | source)
XLA Modules:
  0.0 890.8 jit_solution(7768466526175522370)
XLA Ops:
  0.6 6.2 copy.27
  6.8 5.7 all-to-all-start
  12.5 6.2 copy.30
  18.7 62.9 %all-to-all-done = bf16[4,768,1024]{2,1,0:T(8,128)(2,1)} async-done(((bf16[4,768,1024]{2,1,0:T(8,128)(2,1)}), bf16[4,768,1024]{2,1,0:T(8,128)(2,1)}, u32[]{:S(2)}, u32[]{:S(2)}) %all-to-all-start) | async-done | bytes 6291488 | tf_op jit(solution)/shard_map/all_to_all | solution.py:91
  81.6 6.9 all-to-all-start.2
  88.5 8.6 copy.28
  97.1 60.5 %all-to-all-done.2 = bf16[4,768,1024]{2,1,0:T(8,128)(2,1)} async-done(((bf16[4,768,1024]{2,1,0:T(8,128)(2,1)}), bf16[4,768,1024]{2,1,0:T(8,128)(2,1)}, u32[]{:S(2)}, u32[]{:S(2)}) %all-to-all-start.2) | async-done | bytes 6291488 | tf_op jit(solution)/shard_map/all_to_all | solution.py:92
  157.6 6.2 all-to-all-start.1
  163.8 8.6 copy.31
  172.4 126.3 %all-to-all-done.1 = bf16[768,8,512]{0,2,1:T(8,128)(2,1)} async-done(((bf16[768,8,512]{0,2,1:T(8,128)(2,1)}), bf16[768,8,512]{0,2,1:T(8,128)(2,1)}, u32[]{:S(2)}, u32[]{:S(2)}) %all-to-all-start.1) | async-done | bytes 6291488 | tf_op jit(solution)/shard_map/all_to_all | solution.py:95
  298.7 8.1 all-to-all-start.3
  307.4 11.1 %reshape.139 = bf16[8,2,448,4,128]{4,3,2,1,0:T(4,128)(2,1)} reshape(bf16[7168,512]{1,0:T(8,128)(2,1)} %param.9) | data formatting | bytes 14680064 | tf_op jit(solution)/shard_map/reshape | solution.py:61
  318.5 11.1 %reshape.148 = bf16[8,2,448,4,128]{4,3,2,1,0:T(4,128)(2,1)} reshape(bf16[7168,512]{1,0:T(8,128)(2,1)} %param.10) | data formatting | bytes 14680064 | tf_op jit(solution)/shard_map/reshape | solution.py:62
  329.6 12.8 %reshape.153 = bf16[8,2,384,4,128]{2,1,4,3,0:T(2,128)(2,1)} reshape(bf16[8,768,512]{1,2,0:T(8,128)(2,1)} %bitcast.5) | data formatting | bytes 12582912 | tf_op jit(solution)/shard_map/reshape | solution.py:59
  342.4 98.5 %all-to-all-done.3 = bf16[768,8,512]{0,2,1:T(8,128)(2,1)} async-done(((bf16[768,8,512]{0,2,1:T(8,128)(2,1)}), bf16[768,8,512]{0,2,1:T(8,128)(2,1)}, u32[]{:S(2)}, u32[]{:S(2)}) %all-to-all-start.3) | async-done | bytes 6291488 | tf_op jit(solution)/shard_map/all_to_all | solution.py:96
  440.9 12.8 %reshape.154 = bf16[8,2,384,4,128]{2,1,4,3,0:T(2,128)(2,1)} reshape(bf16[8,768,512]{1,2,0:T(8,128)(2,1)} %bitcast.11) | data formatting | bytes 12582912 | tf_op jit(solution)/shard_map/reshape | solution.py:60
  453.7 184.5 %while.15 = (s32[]{:T(128)}, bf16[8,2,384,4,128]{4,3,2,1,0:T(4,128)(2,1)}, bf16[8,2,448,4,128]{4,3,2,1,0:T(4,128)(2,1)}, bf16[8,2,448,4,128]{4,3,2,1,0:T(4,128)(...) while((s32[]{:T(128)}, ...), condition=%wide.region_3.4_spmd.clone, body=%wide.region_0.3_spmd.clone.sunk | while | flops 2145316480 | bytes 57359940 | solution.py:66
  453.9 1.7 constant_dynamic-slice_fusion.11
  456.7 1.7 constant_dynamic-slice_fusion.13
  464.2 2.4 fusion.46
  468.3 2.4 multiply_convert_fusion.2
  474.1 2.6 copy_dynamic-update-slice_fusion.3
  476.9 1.7 constant_dynamic-slice_fusion.11
  479.8 1.7 constant_dynamic-slice_fusion.13
  487.2 2.4 fusion.46
  491.3 2.4 multiply_convert_fusion.2
  497.2 2.6 copy_dynamic-update-slice_fusion.3
  500.0 1.7 constant_dynamic-slice_fusion.11
  502.8 1.7 constant_dynamic-slice_fusion.13
  510.3 2.4 fusion.46
  514.4 2.4 multiply_convert_fusion.2
  520.2 2.6 copy_dynamic-update-slice_fusion.3
  523.0 1.7 constant_dynamic-slice_fusion.11
  525.9 1.7 constant_dynamic-slice_fusion.13
  533.3 2.4 fusion.46
  537.4 2.4 multiply_convert_fusion.2
  543.3 2.6 copy_dynamic-update-slice_fusion.3
  546.1 1.7 constant_dynamic-slice_fusion.11
  549.0 1.7 constant_dynamic-slice_fusion.13
  556.4 2.4 fusion.46
  560.5 2.4 multiply_convert_fusion.2
  566.3 2.6 copy_dynamic-update-slice_fusion.3
  569.1 1.7 constant_dynamic-slice_fusion.11
  572.0 1.7 constant_dynamic-slice_fusion.13
  579.5 2.4 fusion.46
  583.6 2.4 multiply_convert_fusion.2
  589.4 2.6 copy_dynamic-update-slice_fusion.3
  595.1 1.7 constant_dynamic-slice_fusion.13
  602.5 2.4 fusion.46
  606.6 2.4 multiply_convert_fusion.2
  612.4 2.6 copy_dynamic-update-slice_fusion.3
  618.1 1.7 constant_dynamic-slice_fusion.13
  625.6 2.4 fusion.46
  629.7 2.4 multiply_convert_fusion.2
  635.5 2.6 copy_dynamic-update-slice_fusion.3
  638.1 10.1 %all_to_all.84 = bf16[8,768,512]{2,1,0:T(8,128)(2,1)} reshape(bf16[8,2,384,4,128]{4,3,2,1,0:T(4,128)(2,1)} %get-tuple-element.67) | data formatting | bytes 12582912 | tf_op jit(solution)/shard_map/all_to_all | solution.py:110
  648.3 143.2 %all_to_all.96 = bf16[8,768,512]{2,1,0:T(8,128)(2,1)} all-to-all(bf16[8,768,512]{2,1,0:T(8,128)(2,1)} %all_to_all.84), channel_id=1, replica_groups=mesh['seq'=8,'text'=4] {'seq'}, dimensions={0} | all-to-all | bytes 12582912 | tf_op jit(solution)/shard_map/all_to_all | solution.py:110
  791.5 8.6 copy.38
  800.1 6.8 all-to-all-start.5
  806.9 7.5 copy.72
  814.5 4.3 copy.73
  818.8 57.2 %all-to-all-done.5 = bf16[768,4,1024]{0,2,1:T(8,128)(2,1)} async-done(((bf16[768,4,1024]{0,2,1:T(8,128)(2,1)}), bf16[768,4,1024]{0,2,1:T(8,128)(2,1)}, u32[]{:S(2)}, u32[]{:S(2)}) %all-to-all-start.5) | async-done | bytes 6291488 | tf_op jit(solution)/shard_map/all_to_all | solution.py:109
  876.0 8.6 copy.39
  884.7 6.2 copy.40
  (131 shorter events, 101.3 us)
Async XLA Ops:
  6.8 74.8 %all-to-all-start = ((bf16[4,768,1024]{2,1,0:T(8,128)(2,1)}), bf16[4,768,1024]{2,1,0:T(8,128)(2,1)}, u32[]{:S(2)}, u32[]{:S(2)}) async-start(bf16[4,768,1024]{2,1,0:T(8,128)(2,1)} %bitcast.121), calls=%async_computation | async-start | bytes 12582912 | tf_op jit(solution)/shard_map/all_to_all | solution.py:91
  81.6 75.9 %all-to-all-start.2 = ((bf16[4,768,1024]{2,1,0:T(8,128)(2,1)}), bf16[4,768,1024]{2,1,0:T(8,128)(2,1)}, u32[]{:S(2)}, u32[]{:S(2)}) async-start(bf16[4,768,1024]{2,1,0:T(8,128)(2,1)} %bitcast.119), calls=%async_computation.2 | async-start | bytes 12582912 | tf_op jit(solution)/shard_map/all_to_all | solution.py:92
  157.6 141.1 %all-to-all-start.1 = ((bf16[768,8,512]{0,2,1:T(8,128)(2,1)}), bf16[768,8,512]{0,2,1:T(8,128)(2,1)}, u32[]{:S(2)}, u32[]{:S(2)}) async-start(bf16[768,8,512]{0,2,1:T(8,128)(2,1)} %bitcast.118), calls=%async_computation.1 | async-start | bytes 12582912 | tf_op jit(solution)/shard_map/all_to_all | solution.py:95
  298.7 8.2 copy-start
  298.7 8.2 copy-start.1
  298.7 142.2 %all-to-all-start.3 = ((bf16[768,8,512]{0,2,1:T(8,128)(2,1)}), bf16[768,8,512]{0,2,1:T(8,128)(2,1)}, u32[]{:S(2)}, u32[]{:S(2)}) async-start(bf16[768,8,512]{0,2,1:T(8,128)(2,1)} %bitcast.117), calls=%async_computation.3 | async-start | bytes 12582912 | tf_op jit(solution)/shard_map/all_to_all | solution.py:96
  800.1 14.4 %slice-start = ((s8[7340032]{0:T(1024)(128)(4,1)}), s8[3145728]{0:T(1024)(128)(4,1)S(1)}, s32[]{:S(2)}) async-start(s8[7340032]{0:T(1024)(128)(4,1)} %bitcast.125), calls=%async_computation.6 | async-start | bytes 6291456
  800.1 75.9 %all-to-all-start.5 = ((bf16[768,4,1024]{0,2,1:T(8,128)(2,1)}), bf16[768,4,1024]{0,2,1:T(8,128)(2,1)}, u32[]{:S(2)}, u32[]{:S(2)}) async-start(bf16[768,4,1024]{0,2,1:T(8,128)(2,1)} %bitcast.120), calls=%async_computation.5 | async-start | bytes 12582912 | tf_op jit(solution)/shard_map/all_to_all | solution.py:109
  806.9 7.5 slice-start.1
where the time goes:
time: 899 us; the launch traced here: 891 us
  waiting for transfers between devices  405 us (45%)
  local copies, waits for them, and re-layouts  229 us (25%)
  blocking collectives  143 us (16%)
  matrix products  77.4 us (9%)
  starting transfers between devices  33.8 us (4%)
    all_to_all x1, blocking collectives, body(): lax.all_to_all(far_query_grads, 'seq', split_axis=0, concat_axis=1, tiled...  143 us
    all_to_all x1, waiting for transfers between devices, body(): lax.all_to_all(middle_queries, 'seq', split_axis=1, concat_axis=0, tiled=...  126 us
    all_to_all x1, waiting for transfers between devices, body(): lax.all_to_all(middle_grads, 'seq', split_axis=1, concat_axis=0, tiled=True)  98.5 us
    dynamic_slice x48, local copies, waits for them, and re-layouts, local_backward(): lax.scan(per_group, jnp.zeros((), jnp.float32), shaped)  70 us
    all_to_all x1, waiting for transfers between devices, body(): lax.all_to_all(by_block(queries), 'text', split_axis=0, concat_axis=1, ti...  62.9 us
    all_to_all x1, waiting for transfers between devices, body(): lax.all_to_all(by_block(grad_out), 'text', split_axis=0, concat_axis=1, t...  60.5 us
    all_to_all x1, waiting for transfers between devices, body(): lax.all_to_all(lax.all_to_all(far_query_grads, 'seq', split_axis=0, conca...  57.2 us
    dynamic_update_slice x24, local copies, waits for them, and re-layouts, local_backward(): lax.scan(per_group, jnp.zeros((), jnp.float32), shaped)  35.2 us
  transfers between devices with their start and end apart: 5, of which 5 were waited for; matrix products, arithmetic and copies ran while one was open for 8% of the time, Pallas kernels for 0%

commit v1 on v0

v1 whole, which is shorter than its diff:
```python
import functools
import math

import jax
import jax.numpy as jnp
from jax import lax
from jax.experimental import pallas as pl
from jax.experimental.pallas import tpu as pltpu
from jax.sharding import PartitionSpec as P

HEAD_DIM = 128
LAG = 4


def nt(a, b):
    return lax.dot_general(a, b, (((1,), (1,)), ((), ())), preferred_element_type=jnp.float32)


def tn(a, b):
    return lax.dot_general(a, b, (((0,), (0,)), ((), ())), preferred_element_type=jnp.float32)


def kernel(
    S, T, NB, res, tok, width,
    rows_ref, toks_ref, q_ref, g_ref, k_ref, v_ref,
    dq_ref, dk_ref, dv_ref,
    far, kv, rmid, dqst, dkv,
    kv_sem, dkv_sem, fs, fr, r1s, r1r, r2s, r2r,
):
    R = S // T
    NS = S * NB
    s = lax.axis_index("seq")
    t = lax.axis_index("text")
    z = s // R
    r = s % R
    scale = 1.0 / math.sqrt(HEAD_DIM)

    for w, ref in enumerate((k_ref, v_ref)):
        pltpu.make_async_copy(ref, kv.at[w], kv_sem.at[w]).start()

    barrier = pltpu.get_barrier_semaphore()
    me = s * T + t

    def greet(d, carry):
        other = (me + d) % (S * T)
        pl.semaphore_signal(
            barrier, inc=1, device_id=(other // T, other % T),
            device_id_type=pl.DeviceIdType.MESH,
        )
        return carry

    lax.fori_loop(1, S * T, greet, 0)
    pl.semaphore_wait(barrier, S * T - 1)

    def fwd_refs(w, d, jj):
        rr = (r + d % R) % R
        tt = (t + d // R) % T
        ref = (q_ref, g_ref)[w]
        src = ref.at[jj * T + tt, :, pl.ds(pl.multiple_of(rr * width, 128), width)]
        return src, far.at[w, s * NB + jj], (t * R + rr, tt)

    def fwd_remote(w, d, jj):
        src, dst, dev = fwd_refs(w, d, jj)
        return pltpu.make_async_remote_copy(
            src_ref=src, dst_ref=dst,
            send_sem=fs.at[w, d * NB + jj], recv_sem=fr.at[w, s * NB + jj],
            device_id=dev, device_id_type=pl.DeviceIdType.MESH,
        )

    def fwd_self(d):
        return jnp.logical_and(d == 0, z == t)

    def send_fwd(m, carry):
        jj = m // (R * T)
        d = m % (R * T)
        own = fwd_self(d)

        @pl.when(own)
        def _():
            for w in range(2):
                src, dst, unused = fwd_refs(w, d, jj)
                pltpu.make_async_copy(src, dst, fr.at[w, s * NB + jj]).start()

        @pl.when(jnp.logical_not(own))
        def _():
            for w in range(2):
                fwd_remote(w, d, jj).start()

        return carry

    lax.fori_loop(0, R * T * NB, send_fwd, 0)

    def ret1(zs, rs, jj):
        return pltpu.make_async_remote_copy(
            src_ref=dqst.at[(zs * R + rs) * NB + jj],
            dst_ref=rmid.at[(z * R + rs) * NB + jj],
            send_sem=r1s.at[(zs * R + rs) * NB + jj],
            recv_sem=r1r.at[(z * R + rs) * NB + jj],
            device_id=(zs * R + r, t), device_id_type=pl.DeviceIdType.MESH,
        )

    def ret2_refs(src_buf, zf, rs, jj):
        i = (zf * R + rs) * NB + jj
        dst = dq_ref.at[jj * T + t, :, pl.ds(pl.multiple_of(r * width, 128), width)]
        return src_buf.at[i], dst, r2r.at[(jj * T + t) * R + r]

    def ret2_remote(src_buf, zf, rs, jj):
        src, dst, sem = ret2_refs(src_buf, zf, rs, jj)
        return pltpu.make_async_remote_copy(
            src_ref=src, dst_ref=dst,
            send_sem=r2s.at[(zf * R + rs) * NB + jj], recv_sem=sem,
            device_id=(z * R + rs, zf), device_id_type=pl.DeviceIdType.MESH,
        )

    def ret2_self(zf, rs):
        return jnp.logical_and(rs == r, zf == t)

    def start_ret2(src_buf, zf, rs, jj):
        own = ret2_self(zf, rs)

        @pl.when(own)
        def _():
            src, dst, sem = ret2_refs(src_buf, zf, rs, jj)
            pltpu.make_async_copy(src, dst, sem).start()

        @pl.when(jnp.logical_not(own))
        def _():
            ret2_remote(src_buf, zf, rs, jj).start()

    def order(n):
        jj = n // (T * R)
        hop = (n // R) % T
        return jj, hop, n % R

    def pass_on(n):
        jj, hop, rs = order(n)
        zf = (z + T - hop) % T

        @pl.when(hop != 0)
        def _():
            i = (zf * R + rs) * NB + jj
            pltpu.make_async_copy(rmid.at[i], rmid.at[i], r1r.at[i]).wait()
            start_ret2(rmid, zf, rs, jj)

    for w, ref in enumerate((k_ref, v_ref)):
        pltpu.make_async_copy(ref, kv.at[w], kv_sem.at[w]).wait()

    def out_copy(w, b, i):
        return pltpu.make_async_copy(
            dkv.at[w, b], (dk_ref, dv_ref)[w].at[i], dkv_sem.at[w, b]
        )

    def step(n, carry):
        jj, hop, rs = order(n)
        zs = (z + hop) % T
        i = (zs * R + rs) * NB + jj
        b = n % 2
        for w in range(2):
            pltpu.make_async_copy(far.at[w, i], far.at[w, i], fr.at[w, i]).wait()

        @pl.when(n >= 2)
        def _():
            for w in range(2):
                out_copy(w, b, i).wait()

        tok_ok = lax.broadcasted_iota(jnp.int32, (tok, 1), 0) < toks_ref[i]
        res_ok = lax.broadcasted_iota(jnp.int32, (1, res), 1) < rows_ref[i]
        for h in range(width // HEAD_DIM):
            cols = slice(h * HEAD_DIM, (h + 1) * HEAD_DIM)
            q = far[0, i, :, cols]
            g = far[1, i, :, cols]
            k = kv[0, i, :, cols]
            v = kv[1, i, :, cols]
            raised = jnp.where(tok_ok, jnp.exp(nt(k, q) * scale), 0.0)
            total = jnp.sum(raised, axis=0, keepdims=True)
            attention = raised * jnp.where(res_ok, 1.0 / total, 0.0)
            attention_b = attention.astype(jnp.bfloat16)
            grad_attention = nt(v, g)
            delta = jnp.sum(
                attention_b.astype(jnp.float32) * grad_attention, axis=0, keepdims=True
            )
            scores_b = (scale * attention * (grad_attention - delta)).astype(jnp.bfloat16)
            dkv[0, b, :, cols] = jnp.dot(
                scores_b, q, preferred_element_type=jnp.float32
            ).astype(jnp.bfloat16)
            dkv[1, b, :, cols] = jnp.dot(
                attention_b, g, preferred_element_type=jnp.float32
            ).astype(jnp.bfloat16)
            dqst[i, :, cols] = tn(k, scores_b).T.astype(jnp.bfloat16)

        @pl.when(hop == 0)
        def _():
            start_ret2(dqst, z, rs, jj)

        @pl.when(hop != 0)
        def _():
            ret1(zs, rs, jj).start()

        for w in range(2):
            out_copy(w, b, i).start()

        @pl.when(n >= LAG)
        def _():
            pass_on(n - LAG)

        return carry

    lax.fori_loop(0, NS, step, 0)

    def rest(n, carry):
        pass_on(n)
        return carry

    lax.fori_loop(NS - LAG, NS, rest, 0)

    for b in range(2):
        for w in range(2):
            out_copy(w, b, 0).wait()

    def end_fwd(m, carry):
        jj = m // (R * T)
        d = m % (R * T)

        @pl.when(jnp.logical_not(fwd_self(d)))
        def _():
            for w in range(2):
                fwd_remote(w, d, jj).wait_send()

        return carry

    lax.fori_loop(0, R * T * NB, end_fwd, 0)

    def end_ret(n, carry):
        jj, hop, rs = order(n)
        zs = (z + hop) % T

        @pl.when(hop != 0)
        def _():
            ret1(zs, rs, jj).wait_send()

        zf = (z + T - hop) % T

        @pl.when(jnp.logical_not(ret2_self(zf, rs)))
        def _():
            ret2_remote(rmid, zf, rs, jj).wait_send()

        j = n // R
        place = dq_ref.at[j, :, pl.ds(pl.multiple_of(rs * width, 128), width)]
        pltpu.make_async_copy(place, place, r2r.at[j * R + rs]).wait()
        return carry

    lax.fori_loop(0, NS, end_ret, 0)


def body(queries, keys, values, grad_out, res_len, tok_len):
    S = lax.axis_size("seq")
    T = lax.axis_size("text")
    proteins = res_len.shape[0]
    here = proteins // S
    NB = here // T
    NS = proteins // T
    res = queries.shape[0] // here
    tok = keys.shape[0] // NS
    width = keys.shape[1]
    text_block = lax.axis_index("text")

    def mine(lengths):
        return lax.dynamic_index_in_dim(lengths.reshape(NS, T), text_block, 1, keepdims=False)

    any_spec = pl.BlockSpec(memory_space=pl.ANY)
    smem = pl.BlockSpec(memory_space=pltpu.SMEM)
    dma = pltpu.SemaphoreType.DMA
    bf16 = jnp.bfloat16
    units = NS * (width // HEAD_DIM) * res * tok
    dq, dk, dv = pl.pallas_call(
        functools.partial(kernel, S, T, NB, res, tok, width),
        out_shape=(
            jax.ShapeDtypeStruct((here, res, queries.shape[1]), bf16),
            jax.ShapeDtypeStruct((NS, tok, width), bf16),
            jax.ShapeDtypeStruct((NS, tok, width), bf16),
        ),
        in_specs=[smem, smem, any_spec, any_spec, any_spec, any_spec],
        out_specs=(any_spec, any_spec, any_spec),
        scratch_shapes=[
            pltpu.VMEM((2, NS, res, width), bf16),
            pltpu.VMEM((2, NS, tok, width), bf16),
            pltpu.VMEM((NS, res, width), bf16),
            pltpu.VMEM((NS, res, width), bf16),
            pltpu.VMEM((2, 2, tok, width), bf16),
            dma((2,)),
            dma((2, 2)),
            dma((2, NS)),
            dma((2, NS)),
            dma((NS,)),
            dma((NS,)),
            dma((NS,)),
            dma((NS,)),
        ],
        compiler_params=pltpu.CompilerParams(
            collective_id=0, has_side_effects=True, vmem_limit_bytes=60 * 1024 * 1024
        ),
        cost_estimate=pl.CostEstimate(
            flops=10 * units * HEAD_DIM, bytes_accessed=8 * queries.size * 2, transcendentals=units
        ),
    )(
        mine(res_len),
        mine(tok_len),
        queries.reshape(here, res, -1),
        grad_out.reshape(here, res, -1),
        keys.reshape(NS, tok, width),
        values.reshape(NS, tok, width),
    )
    return (dq.reshape(queries.shape), dk.reshape(keys.shape), dv.reshape(values.shape))


def solution(mesh):
    return jax.shard_map(
        body,
        mesh=mesh,
        in_specs=(P("seq", "text"), P("text", "seq"), P("text", "seq"), P("seq", "text"), P(), P()),
        out_specs=(P("seq", "text"), P("text", "seq"), P("text", "seq")),
        check_vma=False,
    )
```

time: 899 us -> 741 us (0.82)
  Pallas kernels: 0 us -> 708 us
  waiting for transfers between devices: 405 us -> 0 us
  local copies, waits for them, and re-layouts: 229 us -> 18.4 us
  blocking collectives: 143 us -> 0 us
  matrix products: 77.4 us -> 0 us
  starting transfers between devices: 33.8 us -> 0 us
    pallas_call x0 -> x1, Pallas kernels: none -> 708 us  [body(): pl.pallas_call(functools.partial(kernel, S, T, NB, res, tok, width), out_...]
    all_to_all x5 -> x0, waiting for transfers between devices: 405 us -> none  [the longest x1 126 us: body(): lax.all_to_all(middle_queries, 'seq', split_axis=1, concat_axis=0, tiled=...]
    all_to_all x1 -> x0, blocking collectives: 143 us -> none  [body(): lax.all_to_all(far_query_grads, 'seq', split_axis=0, concat_axis=1, tiled...]
    dot_general x48 -> x0, matrix products: 77.4 us -> none  [the longest x8 19.4 us: per_group(): jnp.einsum('ghrt,gthd->grhd', attention_b, value_part, preferred_element_...]
    dynamic_slice x49 -> x1, local copies, waits for them, and re-layouts: 70.2 us -> 0.71 us  [mine(): lax.dynamic_index_in_dim(lengths.reshape(NS, T), text_block, 1, keepdims=...]
    reshape x8 -> x2, local copies, waits for them, and re-layouts: 48.1 us -> 1.48 us  [mine(): lengths.reshape(NS, T)]
    all_to_all x5 -> x0, local copies, waits for them, and re-layouts: 44.6 us -> none  [the longest x2 18.7 us: body(): lax.all_to_all(far_query_grads, 'seq', split_axis=0, concat_axis=1, tiled...]
    dynamic_update_slice x24 -> x0, local copies, waits for them, and re-layouts: 35.2 us -> none  [local_backward(): lax.scan(per_group, jnp.zeros((), jnp.float32), shaped)]
  transfers between devices with their start and end apart: 5 -> 0, of which waited for: 5 -> 0; matrix products, arithmetic and copies ran while one was open for 8% -> 0% of each run, Pallas kernels for 0% -> 0%
where the time goes in v1:
time: 741 us; the launch traced here: 727 us
  Pallas kernels  708 us (96%)
  local copies, waits for them, and re-layouts  18.4 us (2%)
    pallas_call x1, Pallas kernels, body(): pl.pallas_call(functools.partial(kernel, S, T, NB, res, tok, width), out_...  708 us
    unnamed x7, local copies, waits for them, and re-layouts  16.2 us

profile of v1, /device:TPU:14, one launch (start us, length us, event | category | flops | bytes accessed | tf_op | source)
XLA Modules:
  0.0 726.8 jit_solution(15162638516491501933)
XLA Ops:
  0.6 0.7 reshape.33
  1.4 0.7 reshape.34
  2.1 0.7 dynamic-slice_reduce_fusion
  2.8 707.8 %shard_map.85 = (bf16[8,384,1024]{2,1,0:T(8,128)(2,1)}, bf16[16,448,512]{2,1,0:T(8,128)(2,1)}, bf16[16,448,512]{2,1,0:T(8,128)(2,1)}) custom-call(s32[16]{0:T(128)} %get-tuple-element.10.rows_ref, s32[16]{0:T(128)} %get-tuple-element.9.toks_ref, bf16[8,384,1024]{2,1,0:T(8,128)(2,1)} %bitcast.14, bf16[8,384,1024]{2,1,0:T(8,128)(2,1)} %bitcast.15, ...), custom_call_target="tpu_custom_call" | custom-call | flops 14092861440 | bytes 50331648 | tf_op jit(solution)/shard_map/pallas_call | solution.py:275
  710.6 0.0 slice-start
  710.7 6.4 copy.12
  717.0 0.0 slice-start.1
  717.0 6.8 copy.13
  723.8 0.0 slice-done
  723.8 0.0 slice-done.1
  723.8 3.0 copy.14
  (1 shorter events, 0.0 us)
Async XLA Ops:
  710.6 13.2 %slice-start = ((s8[7340032]{0:T(1024)(128)(4,1)}), s8[4194304]{0:T(1024)(128)(4,1)S(1)}, s32[]{:S(2)}) async-start(s8[7340032]{0:T(1024)(128)(4,1)} %bitcast.7), calls=%async_computation | async-start | bytes 8388608
  717.0 6.8 slice-start.1

commit v2 on v1

--- a/solution.py
+++ b/solution.py
@@ -9,7 +9,7 @@
 from jax.sharding import PartitionSpec as P
 
 HEAD_DIM = 128
-LAG = 4
+LAG = 6
 
 
 def nt(a, b):
@@ -24,8 +24,8 @@
     S, T, NB, res, tok, width,
     rows_ref, toks_ref, q_ref, g_ref, k_ref, v_ref,
     dq_ref, dk_ref, dv_ref,
-    far, kv, rmid, dqst, dkv,
-    kv_sem, dkv_sem, fs, fr, r1s, r1r, r2s, r2r,
+    far, fmid, kv, rmid, dqst, dkv,
+    kv_sem, dkv_sem, fs, fr, mr, f2s, r1s, r1r, r2s, r2r,
 ):
     R = S // T
     NS = S * NB
@@ -57,38 +57,82 @@
         tt = (t + d // R) % T
         ref = (q_ref, g_ref)[w]
         src = ref.at[jj * T + tt, :, pl.ds(pl.multiple_of(rr * width, 128), width)]
-        return src, far.at[w, s * NB + jj], (t * R + rr, tt)
-
-    def fwd_remote(w, d, jj):
-        src, dst, dev = fwd_refs(w, d, jj)
+        return src, rr, tt
+
+    def fwd_copy(w, d, jj, dst, sem, plane):
+        src, rr, tt = fwd_refs(w, d, jj)
         return pltpu.make_async_remote_copy(
-            src_ref=src, dst_ref=dst,
-            send_sem=fs.at[w, d * NB + jj], recv_sem=fr.at[w, s * NB + jj],
-            device_id=dev, device_id_type=pl.DeviceIdType.MESH,
-        )
-
-    def fwd_self(d):
-        return jnp.logical_and(d == 0, z == t)
+            src_ref=src, dst_ref=dst, send_sem=fs.at[w, d * NB + jj], recv_sem=sem,
+            device_id=(plane * R + rr, tt), device_id_type=pl.DeviceIdType.MESH,
+        )
+
+    def fwd_far(w, d, jj):
+        i = s * NB + jj
+        return fwd_copy(w, d, jj, far.at[w, i], fr.at[w, i], t)
+
+    def fwd_near(w, d, jj):
+        i = (t * R + r) * NB + jj
+        return fwd_copy(w, d, jj, fmid.at[w, i], mr.at[w, i], z)
 
     def send_fwd(m, carry):
         jj = m // (R * T)
         d = m % (R * T)
-        own = fwd_self(d)
-
-        @pl.when(own)
-        def _():
-            for w in range(2):
-                src, dst, unused = fwd_refs(w, d, jj)
-                pltpu.make_async_copy(src, dst, fr.at[w, s * NB + jj]).start()
-
-        @pl.when(jnp.logical_not(own))
-        def _():
-            for w in range(2):
-                fwd_remote(w, d, jj).start()
+        stays = z == t
+
+        @pl.when(jnp.logical_and(d == 0, stays))
+        def _():
+            for w in range(2):
+                src, rr, tt = fwd_refs(w, d, jj)
+                pltpu.make_async_copy(src, far.at[w, s * NB + jj], fr.at[w, s * NB + jj]).start()
+
+        @pl.when(jnp.logical_xor(d == 0, stays))
+        def _():
+            for w in range(2):
+                fwd_far(w, d, jj).start()
+
+        @pl.when(jnp.logical_and(d != 0, jnp.logical_not(stays)))
+        def _():
+            for w in range(2):
+                fwd_near(w, d, jj).start()
 
         return carry
 
     lax.fori_loop(0, R * T * NB, send_fwd, 0)
+
+    def order(n):
+        jj = n // (T * R)
+        k = (n // R) % T
+        hop = ((k + T - 1) // T) * (T - 1 - k % (T - 1))
+        return jj, hop, n % R
+
+    def fwd2(w, ts, rs, jj):
+        i = (ts * R + rs) * NB + jj
+        o = (z * R + rs) * NB + jj
+        return pltpu.make_async_remote_copy(
+            src_ref=fmid.at[w, i], dst_ref=far.at[w, o],
+            send_sem=f2s.at[w, i], recv_sem=fr.at[w, o],
+            device_id=(ts * R + r, t), device_id_type=pl.DeviceIdType.MESH,
+        )
+
+    def passes(n):
+        jj, hop, rs = order(n)
+        ts = (z + T - hop) % T
+        own = jnp.logical_and(rs == r, ts == t)
+        return jj, rs, ts, jnp.logical_and(hop != 0, jnp.logical_not(own))
+
+    def pass_fwd(n, carry):
+        jj, rs, ts, it_does = passes(n)
+
+        @pl.when(it_does)
+        def _():
+            i = (ts * R + rs) * NB + jj
+            for w in range(2):
+                pltpu.make_async_copy(fmid.at[w, i], fmid.at[w, i], mr.at[w, i]).wait()
+                fwd2(w, ts, rs, jj).start()
+
+        return carry
+
+    lax.fori_loop(0, NS, pass_fwd, 0)
 
     def ret1(zs, rs, jj):
         return pltpu.make_async_remote_copy(
@@ -126,11 +170,6 @@
         @pl.when(jnp.logical_not(own))
         def _():
             ret2_remote(src_buf, zf, rs, jj).start()
-
-    def order(n):
-        jj = n // (T * R)
-        hop = (n // R) % T
-        return jj, hop, n % R
 
     def pass_on(n):
         jj, hop, rs = order(n)
@@ -221,14 +260,26 @@
         jj = m // (R * T)
         d = m % (R * T)
 
-        @pl.when(jnp.logical_not(fwd_self(d)))
-        def _():
-            for w in range(2):
-                fwd_remote(w, d, jj).wait_send()
+        @pl.when(jnp.logical_not(jnp.logical_and(d == 0, z == t)))
+        def _():
+            for w in range(2):
+                fwd_far(w, d, jj).wait_send()
 
         return carry
 
     lax.fori_loop(0, R * T * NB, end_fwd, 0)
+
+    def end_pass(n, carry):
+        jj, rs, ts, it_does = passes(n)
+
+        @pl.when(it_does)
+        def _():
+            for w in range(2):
+                fwd2(w, ts, rs, jj).wait_send()
+
+        return carry
+
+    lax.fori_loop(0, NS, end_pass, 0)
 
     def end_ret(n, carry):
         jj, hop, rs = order(n)
@@ -283,12 +334,15 @@
         out_specs=(any_spec, any_spec, any_spec),
         scratch_shapes=[
             pltpu.VMEM((2, NS, res, width), bf16),
+            pltpu.VMEM((2, NS, res, width), bf16),
             pltpu.VMEM((2, NS, tok, width), bf16),
             pltpu.VMEM((NS, res, width), bf16),
             pltpu.VMEM((NS, res, width), bf16),
             pltpu.VMEM((2, 2, tok, width), bf16),
             dma((2,)),
             dma((2, 2)),
+            dma((2, NS)),
+            dma((2, NS)),
             dma((2, NS)),
             dma((2, NS)),
             dma((NS,)),

time: 741 us -> 474 us (0.64); the launches traced: 727 us -> 474 us
  Pallas kernels: 708 us -> 455 us
    pallas_call x1, Pallas kernels: 708 us -> 455 us  [body(): pl.pallas_call(functools.partial(kernel, S, T, NB, res, tok, width), out_...]
where the time goes in v2:
time: 474 us
  Pallas kernels  455 us (96%)
  local copies, waits for them, and re-layouts  18.4 us (4%)
    pallas_call x1, Pallas kernels, body(): pl.pallas_call(functools.partial(kernel, S, T, NB, res, tok, width), out_...  455 us
    unnamed x7, local copies, waits for them, and re-layouts  16.2 us

profile of v2, /device:TPU:14, one launch (start us, length us, event | category | flops | bytes accessed | tf_op | source)
XLA Modules:
  0.0 473.8 jit_solution(12793291187731637097)
XLA Ops:
  0.6 0.7 reshape.33
  1.4 0.7 reshape.34
  2.1 0.7 dynamic-slice_reduce_fusion
  2.8 454.7 %shard_map.85 = (bf16[8,384,1024]{2,1,0:T(8,128)(2,1)}, bf16[16,448,512]{2,1,0:T(8,128)(2,1)}, bf16[16,448,512]{2,1,0:T(8,128)(2,1)}) custom-call(s32[16]{0:T(128)} %get-tuple-element.10.rows_ref, s32[16]{0:T(128)} %get-tuple-element.9.toks_ref, bf16[8,384,1024]{2,1,0:T(8,128)(2,1)} %bitcast.14, bf16[8,384,1024]{2,1,0:T(8,128)(2,1)} %bitcast.15, ...), custom_call_target="tpu_custom_call" | custom-call | flops 14092861440 | bytes 50331648 | tf_op jit(solution)/shard_map/pallas_call | solution.py:326
  457.6 0.0 slice-start
  457.6 6.4 %copy.12 = bf16[3072,1024]{1,0:T(8,128)(2,1)} copy(bf16[3072,1024]{1,0:T(8,128)(2,1)} %bitcast.11) | data formatting | bytes 12582912
  464.0 0.0 slice-start.1
  464.0 6.8 %copy.13 = bf16[7168,512]{1,0:T(8,128)(2,1)} copy(bf16[7168,512]{1,0:T(8,128)(2,1)} %bitcast.10) | data formatting | bytes 14680064
  470.7 0.0 slice-done
  470.7 0.0 slice-done.1
  470.7 3.0 copy.14
  (1 shorter events, 0.0 us)
Async XLA Ops:
  457.6 13.2 %slice-start = ((s8[7340032]{0:T(1024)(128)(4,1)}), s8[4194304]{0:T(1024)(128)(4,1)S(1)}, s32[]{:S(2)}) async-start(s8[7340032]{0:T(1024)(128)(4,1)} %bitcast.7), calls=%async_computation | async-start | bytes 8388608
  464.0 6.8 %slice-start.1 = ((s8[7340032]{0:T(1024)(128)(4,1)}), s8[3145728]{0:T(1024)(128)(4,1)S(1)}, s32[]{:S(2)}) async-start(s8[7340032]{0:T(1024)(128)(4,1)} %bitcast.7), calls=%async_computation.1 | async-start | bytes 6291456

commit v3 on v2

--- a/solution.py
+++ b/solution.py
@@ -74,9 +74,12 @@
         i = (t * R + r) * NB + jj
         return fwd_copy(w, d, jj, fmid.at[w, i], mr.at[w, i], z)
 
+    def turn(a):
+        return (a % 2) * (T // 2) + a // 2 if T % 2 == 0 else a
+
     def send_fwd(m, carry):
         jj = m // (R * T)
-        d = m % (R * T)
+        d = turn(m // R % T) * R + m % R
         stays = z == t
 
         @pl.when(jnp.logical_and(d == 0, stays))
@@ -115,10 +118,11 @@
         )
 
     def passes(n):
-        jj, hop, rs = order(n)
-        ts = (z + T - hop) % T
+        jj = n // (T * R)
+        rs = n % R
+        ts = (t + T - turn(n // R % T)) % T
         own = jnp.logical_and(rs == r, ts == t)
-        return jj, rs, ts, jnp.logical_and(hop != 0, jnp.logical_not(own))
+        return jj, rs, ts, jnp.logical_and(ts != z, jnp.logical_not(own))
 
     def pass_fwd(n, carry):
         jj, rs, ts, it_does = passes(n)

time: 474 us -> 483 us (1.019)
  Pallas kernels: 455 us -> 464 us
    pallas_call x1, Pallas kernels: 455 us -> 464 us  [body(): pl.pallas_call(functools.partial(kernel, S, T, NB, res, tok, width), out_...]
where the time goes in v3:
time: 483 us
  Pallas kernels  464 us (96%)
  local copies, waits for them, and re-layouts  18.4 us (4%)
    pallas_call x1, Pallas kernels, body(): pl.pallas_call(functools.partial(kernel, S, T, NB, res, tok, width), out_...  464 us
    unnamed x7, local copies, waits for them, and re-layouts  16.2 us

profile of v3, /device:TPU:14, one launch (start us, length us, event | category | flops | bytes accessed | tf_op | source)
XLA Modules:
  0.0 483.0 jit_solution(10709063707389240824)
XLA Ops:
  0.6 0.7 reshape.33
  1.4 0.7 reshape.34
  2.1 0.7 dynamic-slice_reduce_fusion
  2.8 463.9 %shard_map.85 = (bf16[8,384,1024]{2,1,0:T(8,128)(2,1)}, bf16[16,448,512]{2,1,0:T(8,128)(2,1)}, bf16[16,448,512]{2,1,0:T(8,128)(2,1)}) custom-call(s32[16]{0:T(128)} %get-tuple-element.10.rows_ref, s32[16]{0:T(128)} %get-tuple-element.9.toks_ref, bf16[8,384,1024]{2,1,0:T(8,128)(2,1)} %bitcast.14, bf16[8,384,1024]{2,1,0:T(8,128)(2,1)} %bitcast.15, ...), custom_call_target="tpu_custom_call" | custom-call | flops 14092861440 | bytes 50331648 | tf_op jit(solution)/shard_map/pallas_call | solution.py:330
  466.8 0.0 slice-start
  466.8 6.4 %copy.12 = bf16[3072,1024]{1,0:T(8,128)(2,1)} copy(bf16[3072,1024]{1,0:T(8,128)(2,1)} %bitcast.11) | data formatting | bytes 12582912
  473.1 0.0 slice-start.1
  473.1 6.8 %copy.13 = bf16[7168,512]{1,0:T(8,128)(2,1)} copy(bf16[7168,512]{1,0:T(8,128)(2,1)} %bitcast.10) | data formatting | bytes 14680064
  479.9 0.0 slice-done
  479.9 0.0 slice-done.1
  479.9 3.0 copy.14
  (1 shorter events, 0.0 us)
Async XLA Ops:
  466.8 13.2 %slice-start = ((s8[7340032]{0:T(1024)(128)(4,1)}), s8[4194304]{0:T(1024)(128)(4,1)S(1)}, s32[]{:S(2)}) async-start(s8[7340032]{0:T(1024)(128)(4,1)} %bitcast.7), calls=%async_computation | async-start | bytes 8388608
  473.1 6.8 %slice-start.1 = ((s8[7340032]{0:T(1024)(128)(4,1)}), s8[3145728]{0:T(1024)(128)(4,1)S(1)}, s32[]{:S(2)}) async-start(s8[7340032]{0:T(1024)(128)(4,1)} %bitcast.7), calls=%async_computation.1 | async-start | bytes 6291456
